TPU v7x, 32 devices: a whole 2x2x4 slice. The times are simulated.
32 devices in a mesh: group: 2 (over x), member: 16 (over z, y, core).
Axes of the slice: x: 2, y: 2, z: 4, core: 2. Of those that a mesh axis runs over, the one named last changes fastest.
Arguments:
- entities: bfloat16 [16384, 400], P(('group', 'member')), may hold values from -1.796875 to 1.796875
- hub_rows: bfloat16 [128, 400], replicated, may hold values from -1.796875 to 1.796875
- relations: float32 [2112, 400], replicated
- matching: int32 [2], replicated, may hold values from 0 to 1, as said below
- head_index: int32 [512, 256], P(('group', 'member')), may hold values from 0 to 511
- tail_index: int32 [512, 256], P(('group', 'member')), may hold values from 0 to 639
- tile_rel: int32 [512], P(('group', 'member')), may hold values from 0 to 2111
- tile_count: int32 [2, 16], P('group', 'member'), may hold values from 1 to 16, as said below
Outputs:
- new_entities: bfloat16 [16384, 400], P(('group', 'member'))
- new_hub: bfloat16 [128, 400], replicated
Inputs may be any that keep to these rules, and one draw needn't show every extreme that they name: `matching`: a permutation of the partitions. `tile_count`: some device has exactly 16 live tiles.
All inputs are finite; a program needn't handle non-finite values.
Results may differ from a plain program's by a relative error of at most 0.014.
Values may be sent and summed in bfloat16 or wider, within the bound.
A program may use at most 64 MiB of HBM per device.

v0:
```python
import jax
import jax.numpy as jnp
from jax import lax
from jax.sharding import PartitionSpec as P

learn_rate = 0.1
contract_first = (((0,), (0,)), ((), ()))
contract_last = (((1,), (1,)), ((), ()))


def rotate(rows, weight):
    half = rows.shape[1] // 2
    real_part = rows[:, :half]
    imag_part = rows[:, half:]
    w_real = weight[:half]
    w_imag = weight[half:]
    return jnp.concatenate(
        [real_part * w_real - imag_part * w_imag, real_part * w_imag + imag_part * w_real], axis=1
    )


def pullback(grads, weight):
    half = grads.shape[1] // 2
    d_real = grads[:, :half]
    d_imag = grads[:, half:]
    w_real = weight[:half]
    w_imag = weight[half:]
    return jnp.concatenate(
        [d_real * w_real + d_imag * w_imag, d_imag * w_real - d_real * w_imag], axis=1
    )


def tile_grads(head_pick, tail_pick, weight):
    query = rotate(head_pick.astype(jnp.float32), weight).astype(jnp.bfloat16)
    scores = lax.dot_general(query, tail_pick, contract_last, preferred_element_type=jnp.float32)
    top_score = jnp.max(scores, axis=1, keepdims=True)
    expo = jnp.exp(scores - top_score)
    probs = expo / jnp.sum(expo, axis=1, keepdims=True)
    diff = (probs - jnp.eye(scores.shape[0], dtype=jnp.float32)).astype(jnp.bfloat16)
    d_query = jnp.dot(diff, tail_pick, preferred_element_type=jnp.float32)
    d_tail = lax.dot_general(
        diff, query, contract_first, preferred_element_type=jnp.float32
    ).astype(jnp.bfloat16)
    d_head = pullback(d_query, weight).astype(jnp.bfloat16)
    return (d_head, d_tail)


def picker(wanted, group_ids, running, shard_rows):
    block_len = running.shape[0]
    positions = jnp.arange(shard_rows.shape[0], dtype=jnp.int32)
    source_group = positions // block_len
    keep_rows = jnp.any((source_group[:, None] == group_ids[None, :]) & wanted[None, :], axis=1)
    selected = jnp.where(keep_rows[:, None], shard_rows, jnp.zeros_like(shard_rows))
    return jax.ops.segment_sum(selected, positions % block_len, num_segments=block_len)


def shards(entities, hub_rows, relations, matching, head_index, tail_index, tile_rel, tile_count):
    row_total = entities.shape[0]
    my_group = lax.axis_index("group")
    group_ids = jnp.arange(matching.shape[0], dtype=jnp.int32)
    partner = jnp.sum(jnp.where(group_ids == my_group, matching, 0))
    partner_rows = picker(
        group_ids == partner,
        group_ids,
        jnp.zeros_like(entities),
        lax.all_gather(entities, "group", axis=0, tiled=True),
    )
    table = jnp.concatenate([partner_rows, hub_rows], axis=0)
    row_ids = jnp.arange(row_total, dtype=jnp.int32)
    table_ids = jnp.arange(table.shape[0], dtype=jnp.int32)
    tile_total = tile_count[0, 0]

    def one_tile(tile_pos, grads):
        head_ids = lax.dynamic_index_in_dim(head_index, tile_pos, 0, keepdims=False)
        tail_ids = lax.dynamic_index_in_dim(tail_index, tile_pos, 0, keepdims=False)
        rel_id = lax.dynamic_index_in_dim(tile_rel, tile_pos, 0, keepdims=False)
        weight = lax.dynamic_index_in_dim(relations, rel_id, 0, keepdims=False)
        head_hot = (head_ids[:, None] == row_ids[None, :]).astype(jnp.bfloat16)
        tail_hot = (tail_ids[:, None] == table_ids[None, :]).astype(jnp.bfloat16)
        head_pick = jnp.dot(head_hot, entities, preferred_element_type=jnp.float32).astype(
            jnp.bfloat16
        )
        tail_pick = jnp.dot(tail_hot, table, preferred_element_type=jnp.float32).astype(
            jnp.bfloat16
        )
        d_head, d_tail = tile_grads(head_pick, tail_pick, weight)
        head_acc = grads[0] + lax.dot_general(
            head_hot, d_head, contract_first, preferred_element_type=jnp.float32
        )
        tail_acc = grads[1] + lax.dot_general(
            tail_hot, d_tail, contract_first, preferred_element_type=jnp.float32
        )
        return (head_acc, tail_acc)

    start_grads = (jnp.zeros(entities.shape, jnp.float32), jnp.zeros(table.shape, jnp.float32))
    head_acc, tail_acc = lax.fori_loop(0, tile_total, one_tile, start_grads)
    back_rows = tail_acc[:row_total].astype(jnp.bfloat16)
    returned = picker(
        matching == my_group,
        group_ids,
        jnp.zeros_like(back_rows),
        lax.all_gather(back_rows, "group", axis=0, tiled=True),
    ).astype(jnp.float32)
    new_entities = (entities.astype(jnp.float32) - learn_rate * (head_acc + returned)).astype(
        jnp.bfloat16
    )
    hub_part = tail_acc[row_total:]
    hub_sum = lax.psum(hub_part, ("group", "member"))
    new_hub = (hub_rows.astype(jnp.float32) - learn_rate * hub_sum).astype(jnp.bfloat16)
    return (new_entities, new_hub)


def solution(mesh):
    placed = (
        P(("group", "member"), None),
        P(),
        P(),
        P(),
        P(("group", "member"), None),
        P(("group", "member"), None),
        P(("group", "member")),
        P("group", "member"),
    )
    return jax.shard_map(
        shards,
        mesh=mesh,
        in_specs=placed,
        out_specs=(P(("group", "member"), None), P()),
        check_vma=False,
    )
```

profile of v0, /device:TPU:0, one launch (start us, length us, event | category | flops | bytes accessed | tf_op | source)
XLA Modules:
  0.0 310.3 jit_solution(2506123327902799500)
XLA Ops:
  7.3 1.3 fusion.26
  8.5 1.3 iota_compare_fusion.8
  9.9 13.3 %all_gather.6 = bf16[1024,400]{0,1:T(8,128)(2,1)S(1)} all-gather(bf16[512,400]{0,1:T(8,128)(2,1)} %param.10), channel_id=1, replica_groups=mesh['group'=2,'member'=16] {'group'}, dimensions={0}, use_global_device_ids=true | all-gather | bytes 1228800 | tf_op jit(solution)/shard_map/all_gather | solution.py:66
  24.0 5.3 %copy.21 = f32[2112,400]{1,0:T(8,128)} copy(f32[2112,400]{0,1:T(8,128)} %param.12) | data formatting | bytes 6758400
  29.3 6.9 %scatter_custom_fusion = bf16[512,400]{1,0:T(8,128)(2,1)S(1)} fusion(s32[1024]{0:T(1024)S(1)} %bitcast.37, bf16[1024,400]{1,0:T(8,128)(2,1)S(1)} %copy.19, bf16[]{:T(256)} %constant.67.clone.1), kind=kCustom, calls=%fused_computation.43 | custom fusion | flops 409600 | bytes 409602 | tf_op jit(solution)/shard_map/scatter-add | solution.py:54
  36.5 135.0 %while.13 = (s32[]{:T(128)}, f32[512,400]{0,1:T(8,128)S(1)}, f32[640,400]{0,1:T(8,128)S(1)}, s32[]{:T(128)}, s32[16,256]{1,0:T(8,128)}, /*index=5*/bf16[512,400]...) while((s32[]{:T(128)}, f32[512,400]{0,1:T(8,128)S(1)}, ...), condition=%wide.region_6.7_spmd.clone, body=%wide.region_3.6_spmd.clone.sunk | while | flops 633636352 | bytes 9774609 | solution.py:96
  39.7 0.9 constant_dynamic-slice_fusion.6
  40.5 0.7 constant_dynamic-slice_fusion.5
  43.6 1.2 fusion.49
  48.6 0.9 constant_dynamic-slice_fusion.6
  49.5 0.7 constant_dynamic-slice_fusion.5
  51.9 0.7 convolution_add_fusion.5
  52.5 1.2 fusion.49
  57.6 0.9 constant_dynamic-slice_fusion.6
  58.4 0.7 constant_dynamic-slice_fusion.5
  61.5 1.2 fusion.49
  66.5 0.9 constant_dynamic-slice_fusion.6
  67.4 0.7 constant_dynamic-slice_fusion.5
  69.8 0.7 convolution_add_fusion.5
  70.5 1.2 fusion.49
  75.5 0.9 constant_dynamic-slice_fusion.6
  76.3 0.7 constant_dynamic-slice_fusion.5
  79.4 1.2 fusion.49
  84.4 0.9 constant_dynamic-slice_fusion.6
  85.3 0.7 constant_dynamic-slice_fusion.5
  87.7 0.7 convolution_add_fusion.5
  88.4 1.2 fusion.49
  93.4 0.9 constant_dynamic-slice_fusion.6
  94.3 0.7 constant_dynamic-slice_fusion.5
  97.3 1.2 fusion.49
  102.4 0.9 constant_dynamic-slice_fusion.6
  103.2 0.7 constant_dynamic-slice_fusion.5
  105.6 0.7 convolution_add_fusion.5
  106.3 1.2 fusion.49
  111.3 0.9 constant_dynamic-slice_fusion.6
  112.2 0.7 constant_dynamic-slice_fusion.5
  115.3 1.2 fusion.49
  120.3 0.9 constant_dynamic-slice_fusion.6
  121.1 0.7 constant_dynamic-slice_fusion.5
  123.5 0.7 convolution_add_fusion.5
  124.2 1.2 fusion.49
  129.2 0.9 constant_dynamic-slice_fusion.6
  130.1 0.7 constant_dynamic-slice_fusion.5
  133.2 1.2 fusion.49
  138.2 0.9 constant_dynamic-slice_fusion.6
  139.1 0.7 constant_dynamic-slice_fusion.5
  141.5 0.7 convolution_add_fusion.5
  142.1 1.2 fusion.49
  147.2 0.9 constant_dynamic-slice_fusion.6
  148.0 0.7 constant_dynamic-slice_fusion.5
  151.1 1.2 fusion.49
  156.1 0.9 constant_dynamic-slice_fusion.6
  157.0 0.7 constant_dynamic-slice_fusion.5
  160.1 1.2 fusion.49
  165.1 0.9 constant_dynamic-slice_fusion.6
  165.9 0.7 constant_dynamic-slice_fusion.5
  169.0 1.2 fusion.49
  171.5 0.7 slice.30
  172.5 8.6 %all_gather.7 = bf16[1024,400]{0,1:T(8,128)(2,1)S(1)} all-gather(bf16[512,400]{0,1:T(8,128)(2,1)S(1)} %slice.51), channel_id=1, replica_groups=mesh['group'=2,'member'=16] {'group'}, dimensions={0}, use_global_device_ids=true | all-gather | bytes 1228800 | tf_op jit(solution)/shard_map/all_gather | solution.py:102
  181.2 1.3 copy.22
  182.5 7.4 %scatter_custom_fusion.1 = bf16[512,400]{1,0:T(8,128)(2,1)S(1)} fusion(s32[1024]{0:T(1024)S(1)} %bitcast.38, bf16[1024,400]{1,0:T(8,128)(2,1)} %copy.22, bf16[]{:T(256)} %constant.67.clone.1), kind=kCustom, calls=%fused_computation.41 | custom fusion | flops 409600 | bytes 410112 | tf_op jit(solution)/shard_map/scatter-add | solution.py:54
  190.5 0.9 copy.24
  191.4 110.4 %all-reduce.2.cloned.1.call-done = f32[128,400]{0,1:T(8,128)} async-done(((f32[128,400]{0,1:T(8,128)}), f32[128,400]{0,1:T(8,128)}) %all-reduce.2.cloned.1.call-update) | async-done | bytes 204816 | tf_op jit(solution)/shard_map/psum | solution.py:108
  301.9 1.6 subtract_convert_fusion.7
  (181 shorter events, 51.1 us)
Async XLA Ops:
  7.2 16.7 %copy-start.1 = (bf16[128,400]{0,1:T(8,128)(2,1)S(1)}, bf16[128,400]{0,1:T(8,128)(2,1)}, u32[]{:S(2)}) copy-start(bf16[128,400]{0,1:T(8,128)(2,1)} %param.11) | copy-start | bytes 307204
  7.2 294.7 %all-reduce.2.cloned.1.call-start = ((), (), s32[]{:S(2)}) async-start(), calls=%async_computation | async-start | bytes 409600 | tf_op jit(solution)/shard_map/psum | solution.py:108
  29.3 7.2 %copy-start = (bf16[512,400]{0,1:T(8,128)(2,1)S(1)}, bf16[512,400]{0,1:T(8,128)(2,1)}, u32[]{:S(2)}) copy-start(bf16[512,400]{0,1:T(8,128)(2,1)} %param.10) | copy-start | bytes 1228804
  29.3 7.2 %copy-start.2 = (s32[16]{0:T(128)S(1)}, s32[16]{0:T(128)}, u32[]{:S(2)}) copy-start(s32[16]{0:T(128)} %param.16) | copy-start | bytes 196
  42.2 0.7 copy-start.3
  51.2 0.7 copy-start.3
  60.1 0.7 copy-start.3
  69.1 0.7 copy-start.3
  78.1 0.7 copy-start.3
  87.0 0.7 copy-start.3
  96.0 0.7 copy-start.3
  104.9 0.7 copy-start.3
  113.9 0.7 copy-start.3
  122.9 0.7 copy-start.3
  131.8 0.7 copy-start.3
  140.8 0.7 copy-start.3
  149.7 0.7 copy-start.3
  158.7 0.7 copy-start.3
  167.7 0.7 copy-start.3
Sparse Core Ops, SparseCore 0:
  172.3 129.4 all-reduce.1
where the time goes:
time: 315 us; the launch traced here: 310 us
  waiting for transfers between devices  110 us (35%)
  matrix products  52.6 us (17%)
  local copies, waits for them, and re-layouts  46.5 us (15%)
  loops' own time  40.7 us (13%)
  other arithmetic  23.9 us (8%)
  blocking collectives  21.9 us (7%)
  between operations  14.2 us (5%)
    psum x1, waiting for transfers between devices, shards(): hub_sum = lax.psum(hub_part, ('group', 'member'))  110 us
    another operation x1, loops' own time, shards(): head_acc, tail_acc = lax.fori_loop(0, tile_total, one_tile, start_grads)  40.7 us
    dot_general x15, matrix products, tile_grads(): d_query = jnp.dot(diff, tail_pick, preferred_element_type=jnp.float32)  17.5 us
    scatter-add x2, other arithmetic, picker(): jax.ops.segment_sum(selected, positions % block_len, num_segments=block_len)  14.3 us
    all_gather x1, blocking collectives, shards(): lax.all_gather(entities, 'group', axis=0, tiled=True)  13.3 us
    slice x15, local copies, waits for them, and re-layouts, rotate(): w_real = weight[:half]  12.9 us
    dynamic_slice x15, local copies, waits for them, and re-layouts, one_tile(): tail_ids = lax.dynamic_index_in_dim(tail_index, tile_pos, 0, keepdims=False)  10.8 us
    dot_general x15, matrix products, one_tile(): lax.dot_general(tail_hot, d_tail, contract_first, preferred_element_type=...  9.93 us
  transfers between devices with their start and end apart: 1, of which 1 were waited for; matrix products, arithmetic and copies ran while one was open for 3% of the time, Pallas kernels for 0%

commit v1 on v0

v1 whole, which is shorter than its diff:
```python
import functools

import jax
import jax.numpy as jnp
from jax import lax
from jax.experimental import pallas as pl
from jax.experimental.pallas import tpu as pltpu
from jax.sharding import PartitionSpec as P

learn_rate = 0.1
MESH = pl.DeviceIdType.MESH
LANES = 128
HALF = 256
WIDE = 2 * HALF
CHUNKS = 16
CHUNK_ROWS = 16
contract_first = (((0,), (0,)), ((), ()))
contract_last = (((1,), (1,)), ((), ()))
f32 = jnp.float32
bf16 = jnp.bfloat16


def widen(rows):
    half = rows.shape[1] // 2
    gap = jnp.zeros((rows.shape[0], HALF - half), rows.dtype)
    return jnp.concatenate([rows[:, :half], gap, rows[:, half:], gap], axis=1)


def narrow(rows, half):
    return jnp.concatenate([rows[:, :half], rows[:, HALF : HALF + half]], axis=1)


def fold(rest):
    rows, k = rest.shape
    parts = LANES // k
    step = rows // parts
    return jnp.concatenate([rest[i * step : (i + 1) * step] for i in range(parts)], axis=1)


def unfold(folded, k):
    return jnp.concatenate(
        [folded[:, i * k : (i + 1) * k] for i in range(LANES // k)], axis=0
    )


def kernel(
    groups, members, count_ref, rel_ref, match_ref,
    ent_ref, hub_ref, head_ref, tail_ref, table_ref,
    new_ent_ref, new_hub_ref,
    weights_all, ent_wide, tab_wide, hub_wide, peer_main, peer_rest, rest_send,
    head_col, tail_col, head_row, tail_row, weights, query, d_head, d_tail,
    back_main, back_rest, back_sum, hub_send, hub_in, hub_mid, hub_out,
    rel_sem, ent_send, ent_recv, back_send, back_recv,
    s1, r1, s2, r2, s3, r3,
):
    g = lax.axis_index("group")
    m = lax.axis_index("member")
    rows, width = ent_ref.shape
    half = width // 2
    hub_rows = hub_ref.shape[0]
    tiles, edge = head_ref.shape
    main = width // LANES * LANES
    rest = width - main
    parts = back_send.shape[0]
    part_rows = rows // parts
    part_rest = part_rows * rest // LANES

    load = pltpu.make_async_copy(table_ref, weights_all, rel_sem)
    load.start()
    other_groups = [lax.rem(g + d, groups) for d in range(1, groups)]
    other_members = [lax.rem(m + d, members) for d in range(1, members)]
    barrier = pltpu.get_barrier_semaphore()
    for o in other_groups:
        pl.semaphore_signal(barrier, inc=1, device_id=(o, m), device_id_type=MESH)
    for o in other_members:
        pl.semaphore_signal(barrier, inc=1, device_id=(g, o), device_id_type=MESH)

    rest_send[...] = fold(ent_ref[:, main:].astype(f32)).astype(bf16)
    pl.semaphore_wait(barrier, groups + members - 2)

    def remote(src, dst, send, recv, where):
        return pltpu.make_async_remote_copy(
            src_ref=src, dst_ref=dst, send_sem=send, recv_sem=recv,
            device_id=where, device_id_type=MESH,
        )

    sends = []
    for o in other_groups:
        sends.append(
            remote(ent_ref.at[:, pl.ds(0, main)], peer_main.at[g],
                   ent_send.at[0, o], ent_recv.at[0, g], (o, m)))
        sends.append(
            remote(rest_send, peer_rest.at[g], ent_send.at[1, o], ent_recv.at[1, g], (o, m)))
    for copy in sends:
        copy.start()

    own = ent_ref[...]
    peer_main[g] = own[:, :main]
    peer_rest[g] = rest_send[...]
    ent_wide[...] = widen(own.astype(f32)).astype(bf16)
    hub_w = widen(hub_ref[...].astype(f32))
    tab_wide[pl.ds(rows, hub_rows), :] = hub_w.astype(bf16)
    for c in range(CHUNKS):
        r, k = c // 2 * CHUNK_ROWS, c % 2 * HALF
        hub_wide[c] = hub_w[r : r + CHUNK_ROWS, k : k + HALF]
    heads, tails = head_ref[...], tail_ref[...]
    heads_t, tails_t = heads.T, tails.T
    for t in range(tiles):
        head_col[t] = heads_t[:, t : t + 1]
        tail_col[t] = tails_t[:, t : t + 1]
        head_row[:, t * edge : (t + 1) * edge] = heads[t : t + 1]
        tail_row[:, t * edge : (t + 1) * edge] = tails[t : t + 1]

    load.wait()
    live = count_ref[0, 0]
    picked = []
    for t in range(tiles):
        row = weights_all[pl.ds(rel_ref[t], 1), :]
        picked.append(jnp.where(t < live, row, jnp.zeros_like(row)))
    weights[...] = widen(jnp.concatenate(picked, axis=0))

    def hot(col, n):
        return (col == lax.broadcasted_iota(jnp.int32, (edge, n), 1)).astype(f32).astype(bf16)

    def make_query(t):
        head = jnp.dot(hot(head_col[t], rows), ent_wide[...], preferred_element_type=f32)
        w = weights[pl.ds(t, 1), :]
        wr, wi = w[:, :HALF], w[:, HALF:]
        hr, hi = head[:, :HALF], head[:, HALF:]
        query[t] = jnp.concatenate([hr * wr - hi * wi, hr * wi + hi * wr], axis=1).astype(bf16)

    def query_pair(i, _):
        make_query(2 * i)
        make_query(2 * i + 1)
        return 0

    lax.fori_loop(0, tiles // 2, query_pair, 0)

    for o in other_groups:
        remote(ent_ref.at[:, pl.ds(0, main)], peer_main.at[o],
               ent_send.at[0, o], ent_recv.at[0, o], (o, m)).wait_recv()
        remote(rest_send, peer_rest.at[o],
               ent_send.at[1, o], ent_recv.at[1, o], (o, m)).wait_recv()
    partner = match_ref[g]
    got = jnp.concatenate(
        [peer_main[partner].astype(f32), unfold(peer_rest[partner].astype(f32), rest)], axis=1)
    tab_wide[pl.ds(0, rows), :] = widen(got).astype(bf16)

    def one_tile(t):
        tail = jnp.dot(
            hot(tail_col[t], rows + hub_rows), tab_wide[...], preferred_element_type=f32
        ).astype(bf16)
        q = query[t]
        scores = lax.dot_general(q, tail, contract_last, preferred_element_type=f32)
        expo = jnp.exp(scores - jnp.max(scores, axis=1, keepdims=True))
        probs = expo * (1.0 / jnp.sum(expo, axis=1, keepdims=True))
        eye = lax.broadcasted_iota(jnp.int32, (edge, edge), 0) == lax.broadcasted_iota(
            jnp.int32, (edge, edge), 1)
        diff = jnp.where(eye, probs - 1.0, probs).astype(bf16)
        dq = jnp.dot(diff, tail, preferred_element_type=f32)
        here = pl.ds(pl.multiple_of(t * edge, edge), edge)
        d_tail[here, :] = lax.dot_general(
            diff, q, contract_first, preferred_element_type=f32).astype(bf16)
        w = weights[pl.ds(t, 1), :]
        wr, wi = w[:, :HALF], w[:, HALF:]
        dr, di = dq[:, :HALF], dq[:, HALF:]
        d_head[here, :] = jnp.concatenate(
            [dr * wr + di * wi, di * wr - dr * wi], axis=1).astype(bf16)

    def tile_pair(i, _):
        one_tile(2 * i)
        one_tile(2 * i + 1)
        return 0

    lax.fori_loop(0, tiles // 2, tile_pair, 0)

    def scatter(ids, low, n, grads):
        hot_t = (ids == lax.broadcasted_iota(jnp.int32, (n, tiles * edge), 0) + low)
        return jnp.dot(hot_t.astype(f32).astype(bf16), grads, preferred_element_type=f32)

    def send_back(part, acc):
        low = part * part_rows
        flat = narrow(acc, half)
        back_main[g, low : low + part_rows, :] = flat[:, :main].astype(bf16)
        back_rest[g, part * part_rest : (part + 1) * part_rest, :] = fold(flat[:, main:]).astype(bf16)
        for copy in back_copies(part, g):
            copy.start()

    def back_copies(part, slot):
        out = []
        a = pl.ds(part * part_rows, part_rows)
        b = pl.ds(part * part_rest, part_rest)
        for o in other_groups:
            at = g if slot is g else o
            out.append(remote(back_main.at[at, a], back_main.at[at, a],
                              back_send.at[part, 0, o], back_recv.at[part, 0, at], (o, m)))
            out.append(remote(back_rest.at[at, b], back_rest.at[at, b],
                              back_send.at[part, 1, o], back_recv.at[part, 1, at], (o, m)))
        return out

    last = parts - 1
    acc = scatter(tail_row[...], last * part_rows, part_rows + hub_rows, d_tail[...])
    hub_acc = acc[part_rows:]
    for c in range(CHUNKS):
        r, k = c // 2 * CHUNK_ROWS, c % 2 * HALF
        hub_send[c] = hub_acc[r : r + CHUNK_ROWS, k : k + HALF].astype(bf16)

    owner = m < CHUNKS

    def stage_one(o):
        return remote(hub_send.at[o], hub_in.at[m], s1.at[o], r1.at[m], (g, o))

    for o in other_members:
        @pl.when(o < CHUNKS)
        def _(o=o):
            stage_one(o).start()

    @pl.when(owner)
    def _():
        hub_in[m] = hub_send[m]

    send_back(last, acc[:part_rows])
    for part in range(last):
        send_back(part, scatter(tail_row[...], part * part_rows, part_rows, d_tail[...]))

    def stage_two(o, at):
        return remote(hub_mid.at[at], hub_mid.at[at], s2.at[o], r2.at[at], (o, m))

    @pl.when(owner)
    def _():
        for o in other_members:
            remote(hub_send.at[m], hub_in.at[o], s1.at[o], r1.at[o], (g, o)).wait_recv()
        total = hub_in[0].astype(f32)
        for i in range(1, members):
            total = total + hub_in[i].astype(f32)
        hub_mid[g] = total
        for o in other_groups:
            stage_two(o, g).start()

    back_sum[...] = scatter(head_row[...], 0, rows, d_head[...])

    def stage_three(o, at):
        return remote(hub_out.at[at], hub_out.at[at], s3.at[o], r3.at[at], (g, o))

    @pl.when(owner)
    def _():
        for o in other_groups:
            stage_two(o, o).wait_recv()
        total = hub_mid[0]
        for i in range(1, groups):
            total = total + hub_mid[i]
        hub_out[m] = (hub_wide[m] - learn_rate * total).astype(bf16)
        for o in other_members:
            stage_three(o, m).start()

    for part in [last, *range(last)]:
        for copy in back_copies(part, None):
            copy.wait_recv()
    source = jnp.int32(0)
    for i in range(1, groups):
        source = jnp.where(match_ref[i] == g, i, source)
    for part in [last, *range(last)]:
        low = part * part_rows
        returned = jnp.concatenate(
            [
                back_main[source, low : low + part_rows, :].astype(f32),
                unfold(back_rest[source, part * part_rest : (part + 1) * part_rest, :].astype(f32), rest),
            ],
            axis=1,
        )
        grads = narrow(back_sum[low : low + part_rows, :], half) + returned
        new_ent_ref[low : low + part_rows, :] = (
            ent_ref[low : low + part_rows, :].astype(f32) - learn_rate * grads).astype(bf16)

    for o in other_members:
        @pl.when(o < CHUNKS)
        def _(o=o):
            stage_three(o, o).wait_recv()
    for r in range(CHUNKS // 2):
        pair = jnp.concatenate([hub_out[2 * r].astype(f32), hub_out[2 * r + 1].astype(f32)], axis=1)
        new_hub_ref[r * CHUNK_ROWS : (r + 1) * CHUNK_ROWS, :] = narrow(pair, half).astype(bf16)

    for copy in sends:
        copy.wait_send()
    for part in range(parts):
        for copy in back_copies(part, g):
            copy.wait_send()
    for o in other_members:
        @pl.when(o < CHUNKS)
        def _(o=o):
            stage_one(o).wait_send()

    @pl.when(owner)
    def _():
        for o in other_groups:
            stage_two(o, g).wait_send()
        for o in other_members:
            stage_three(o, m).wait_send()


def shards(groups, members, entities, hub_rows, relations, matching, head_index, tail_index, tile_rel, tile_count):
    rows, width = entities.shape
    hubs = hub_rows.shape[0]
    tiles, edge = head_index.shape
    main = width // LANES * LANES
    folded = rows * (width - main) // LANES
    parts = 2
    smem = pl.BlockSpec(memory_space=pltpu.SMEM)
    vmem = pl.BlockSpec(memory_space=pltpu.VMEM)
    dma = pltpu.SemaphoreType.DMA
    return pl.pallas_call(
        functools.partial(kernel, groups, members),
        out_shape=(
            jax.ShapeDtypeStruct(entities.shape, bf16),
            jax.ShapeDtypeStruct(hub_rows.shape, bf16),
        ),
        in_specs=[smem, smem, smem, vmem, vmem, vmem, vmem, pl.BlockSpec(memory_space=pl.ANY)],
        out_specs=(vmem, vmem),
        scratch_shapes=[
            pltpu.VMEM(relations.shape, f32),
            pltpu.VMEM((rows, WIDE), bf16),
            pltpu.VMEM((rows + hubs, WIDE), bf16),
            pltpu.VMEM((CHUNKS, CHUNK_ROWS, HALF), f32),
            pltpu.VMEM((groups, rows, main), bf16),
            pltpu.VMEM((groups, folded, LANES), bf16),
            pltpu.VMEM((folded, LANES), bf16),
            pltpu.VMEM((tiles, edge, 1), jnp.int32),
            pltpu.VMEM((tiles, edge, 1), jnp.int32),
            pltpu.VMEM((1, tiles * edge), jnp.int32),
            pltpu.VMEM((1, tiles * edge), jnp.int32),
            pltpu.VMEM((tiles, WIDE), f32),
            pltpu.VMEM((tiles, edge, WIDE), bf16),
            pltpu.VMEM((tiles * edge, WIDE), bf16),
            pltpu.VMEM((tiles * edge, WIDE), bf16),
            pltpu.VMEM((groups, rows, main), bf16),
            pltpu.VMEM((groups, folded, LANES), bf16),
            pltpu.VMEM((rows, WIDE), f32),
            pltpu.VMEM((CHUNKS, CHUNK_ROWS, HALF), bf16),
            pltpu.VMEM((members, CHUNK_ROWS, HALF), bf16),
            pltpu.VMEM((groups, CHUNK_ROWS, HALF), f32),
            pltpu.VMEM((CHUNKS, CHUNK_ROWS, HALF), bf16),
            dma,
            dma((2, groups)),
            dma((2, groups)),
            dma((parts, 2, groups)),
            dma((parts, 2, groups)),
            dma((members,)),
            dma((members,)),
            dma((groups,)),
            dma((groups,)),
            dma((members,)),
            dma((members,)),
        ],
        compiler_params=pltpu.CompilerParams(
            collective_id=0, has_side_effects=True, vmem_limit_bytes=56 * 1024 * 1024
        ),
        cost_estimate=pl.CostEstimate(
            flops=4 * tiles * edge * WIDE * (2 * rows + hubs + edge), bytes_accessed=relations.size * 4,
            transcendentals=tiles * edge * edge),
    )(tile_count, tile_rel, matching, entities, hub_rows, head_index, tail_index, relations)


def solution(mesh):
    placed = (
        P(("group", "member"), None),
        P(),
        P(),
        P(),
        P(("group", "member"), None),
        P(("group", "member"), None),
        P(("group", "member")),
        P("group", "member"),
    )
    return jax.shard_map(
        functools.partial(shards, mesh.shape["group"], mesh.shape["member"]),
        mesh=mesh,
        in_specs=placed,
        out_specs=(P(("group", "member"), None), P()),
        check_vma=False,
    )
```

time: 315 us -> 65.8 us (0.21); the launches traced: 310 us -> 65.5 us
  waiting for transfers between devices: 110 us -> 0 us
  matrix products: 52.6 us -> 0 us
  Pallas kernels: 0 us -> 51.6 us
  loops' own time: 40.7 us -> 0 us
  local copies, waits for them, and re-layouts: 46.5 us -> 12.5 us
  other arithmetic: 23.9 us -> 0 us
  blocking collectives: 21.9 us -> 0 us
  between operations: 14.2 us -> 1.29 us
    psum x1 -> x0, waiting for transfers between devices: 110 us -> none  [shards(): hub_sum = lax.psum(hub_part, ('group', 'member'))]
    dot_general x90 -> x0, matrix products: 52.6 us -> none  [the longest x15 17.5 us: tile_grads(): d_query = jnp.dot(diff, tail_pick, preferred_element_type=jnp.float32)]
    pallas_call x0 -> x1, Pallas kernels: none -> 51.6 us  [shards(): pl.pallas_call(functools.partial(kernel, groups, members), out_shape=(jax...]
    another operation x1 -> x0, loops' own time: 40.7 us -> none  [shards(): head_acc, tail_acc = lax.fori_loop(0, tile_total, one_tile, start_grads)]
    all_gather x2 -> x0, blocking collectives: 21.9 us -> none  [the longest x1 13.3 us: shards(): lax.all_gather(entities, 'group', axis=0, tiled=True)]
    dynamic_slice x30 -> x0, local copies, waits for them, and re-layouts: 19.6 us -> none  [the longest x15 10.8 us: one_tile(): tail_ids = lax.dynamic_index_in_dim(tail_index, tile_pos, 0, keepdims=False)]
    scatter-add x2 -> x0, other arithmetic: 14.3 us -> none  [picker(): jax.ops.segment_sum(selected, positions % block_len, num_segments=block_len)]
    slice x17 -> x0, local copies, waits for them, and re-layouts: 13.7 us -> none  [the longest x15 12.9 us: rotate(): w_real = weight[:half]]
  transfers between devices with their start and end apart: 1 -> 0, of which waited for: 1 -> 0; matrix products, arithmetic and copies ran while one was open for 3% -> 0% of each run, Pallas kernels for 0% -> 0%
where the time goes in v1:
time: 65.8 us; the launch traced here: 65.5 us
  Pallas kernels  51.6 us (78%)
  local copies, waits for them, and re-layouts  12.5 us (19%)
  between operations  1.29 us (2%)
    pallas_call x1, Pallas kernels, shards(): pl.pallas_call(functools.partial(kernel, groups, members), out_shape=(jax...  51.6 us
    unnamed x3, local copies, waits for them, and re-layouts  8.91 us
    pallas_call x2, local copies, waits for them, and re-layouts, shards(): pl.pallas_call(functools.partial(kernel, groups, members), out_shape=(jax...  3.63 us

profile of v1, /device:TPU:0, one launch (start us, length us, event | category | flops | bytes accessed | tf_op | source)
XLA Modules:
  0.0 65.5 jit_solution(17196655795479087292)
XLA Ops:
  1.3 1.7 %copy.11.hub_ref = bf16[128,400]{1,0:T(8,128)(2,1)} copy(bf16[128,400]{0,1:T(8,128)(2,1)} %param.9) | data formatting | bytes 204800 | tf_op args[1]
  2.9 2.0 %copy.10.ent_ref = bf16[512,400]{1,0:T(8,128)(2,1)} copy(bf16[512,400]{0,1:T(8,128)(2,1)} %param.8) | data formatting | bytes 819200 | tf_op args[0]
  5.0 5.2 %copy.12.table_ref = f32[2112,400]{1,0:T(8,128)} copy(f32[2112,400]{0,1:T(8,128)} %param.10) | data formatting | bytes 6758400 | tf_op args[2]
  10.2 51.6 %shard_map.95 = (bf16[512,400]{1,0:T(8,128)(2,1)}, bf16[128,400]{1,0:T(8,128)(2,1)}) custom-call(s32[1,1]{1,0:T(1,128)S(6)} %copy.15.count_ref, s32[16]{0:T(128)} %rel_ref.1, s32[2]{0:T(128)} %match_ref.1, bf16[512,400]{1,0:T(8,128)(2,1)} %copy.10.ent_ref, bf16[128,400]{1,0:T(8,128)(2,1)} %copy.11.hub_ref, s32[16,256]{1,0:T(8,128)} %head_ref.1, ...), custom_call_target="tpu_custom_call" | custom-call | flops 11811160064 | bytes 3379200 | tf_op jit(solution)/shard_map/pallas_call | solution.py:311
  61.8 2.0 %copy.13 = bf16[512,400]{0,1:T(8,128)(2,1)} copy(bf16[512,400]{1,0:T(8,128)(2,1)} %get-tuple-element.2) | data formatting | bytes 819200 | tf_op jit(solution)/shard_map/pallas_call | solution.py:311
  63.8 1.7 %copy.14 = bf16[128,400]{0,1:T(8,128)(2,1)} copy(bf16[128,400]{1,0:T(8,128)(2,1)} %get-tuple-element.3) | data formatting | bytes 204800 | tf_op jit(solution)/shard_map/pallas_call | solution.py:311

commit v2 on v1

v2 whole, which is shorter than its diff:
```python
import functools

import jax
import jax.numpy as jnp
from jax import lax
from jax.experimental import pallas as pl
from jax.experimental.pallas import tpu as pltpu
from jax.sharding import PartitionSpec as P

learn_rate = 0.1
MESH = pl.DeviceIdType.MESH
LANES = 128
CHUNK_ROWS = 32
contract_last = (((1,), (1,)), ((), ()))
f32 = jnp.float32
bf16 = jnp.bfloat16


def dot(a, b):
    return jnp.dot(a, b, preferred_element_type=f32)


def dot_last(a, b):
    return lax.dot_general(a, b, contract_last, preferred_element_type=f32)


def kernel(
    groups, members, count_ref, rel_ref, match_ref,
    ent_ref, hub_ref, head_ref, tail_ref, table_ref,
    new_ent_ref, new_hub_ref,
    landed, relations, peers_0, peers_1, table, weights, hot_head, hot_tail, picked,
    query_t, query, d_head, d_tail, back_0, back_1, head_sum,
    hub_pad, hub_send, hub_in, hub_mid, hub_out,
    rel_sem, ent_send, ent_recv, back_send, back_recv,
    s1, r1, s2, r2, s3, r3,
):
    g = lax.axis_index("group")
    m = lax.axis_index("member")
    width, rows = ent_ref.shape
    half = width // 2
    hubs = hub_ref.shape[1]
    tiles, edge = head_ref.shape
    rels = table_ref.shape[1]
    peers, back = (peers_0, peers_1), (back_0, back_1)
    parts = len(back)
    part_rows = rows // parts
    chunks = hub_send.shape[0]

    blocks = relations.shape[0]
    load = pltpu.make_async_copy(table_ref, landed, rel_sem)
    load.start()
    other_groups = [lax.rem(g + d, groups) for d in range(1, groups)]
    other_members = [lax.rem(m + d, members) for d in range(1, members)]
    barrier = pltpu.get_barrier_semaphore()
    for o in other_groups:
        pl.semaphore_signal(barrier, inc=1, device_id=(o, m), device_id_type=MESH)
    for o in other_members:
        pl.semaphore_signal(barrier, inc=1, device_id=(g, o), device_id_type=MESH)
    pl.semaphore_wait(barrier, groups + members - 2)

    def remote(src, dst, send, recv, where):
        return pltpu.make_async_remote_copy(
            src_ref=src, dst_ref=dst, send_sem=send, recv_sem=recv,
            device_id=where, device_id_type=MESH,
        )

    def lanes_of(part):
        return pl.ds(part * part_rows, part_rows)

    def ent_copy(part, o, slot):
        return remote(ent_ref.at[:, lanes_of(part)], peers[part].at[slot],
                      ent_send.at[part, o], ent_recv.at[part, slot], (o, m))

    for part in range(parts):
        for o in other_groups:
            ent_copy(part, o, g).start()

    for part in range(parts):
        peers[part][g] = ent_ref[:, lanes_of(part)]
    hub_now = hub_ref[...].astype(f32)
    for c in range(chunks):
        piece = hub_now[c * CHUNK_ROWS : (c + 1) * CHUNK_ROWS]
        hub_pad[c, : piece.shape[0], :] = piece
        if piece.shape[0] < CHUNK_ROWS:
            hub_pad[c, piece.shape[0] :, :] = jnp.zeros(
                (CHUNK_ROWS - piece.shape[0], hubs), f32)
    load.wait()
    for i in range(blocks):
        piece = landed[:, i * LANES : (i + 1) * LANES]
        if piece.shape[1] < LANES:
            piece = jnp.concatenate(
                [piece, jnp.zeros((width, LANES - piece.shape[1]), f32)], axis=1)
        relations[i] = piece
    live = count_ref[0, 0]
    lane = lax.broadcasted_iota(jnp.int32, (width, LANES), 1)

    def lanes_at(t):
        return pl.ds(pl.multiple_of(t * edge, edge), edge)

    def hot(ids, n):
        return (lax.broadcasted_iota(jnp.int32, (n, edge), 0) == ids).astype(f32).astype(bf16)

    def weight_of(t):
        rel = rel_ref[t]
        block = jnp.int32(0)
        for i in range(1, blocks):
            block = jnp.where(rel >= i * LANES, i, block)
        kept = jnp.where(lane == rel - block * LANES, relations[block], 0.0)
        column = jnp.sum(kept, axis=1, keepdims=True)
        column = jnp.where(t < live, column, jnp.zeros_like(column))
        weights[t] = jnp.broadcast_to(column, (width, LANES))

    def halves(t):
        w = jnp.concatenate([weights[t]] * (edge // LANES), axis=1)
        return w[:half], w[half:]

    def prepare(t):
        at = lanes_at(t)
        hot_h = hot(head_ref[pl.ds(t, 1), :], rows)
        hot_head[:, at] = hot_h
        head = dot(ent_ref[...], hot_h)
        wr, wi = halves(t)
        hr, hi = head[:half], head[half:]
        q = jnp.concatenate([hr * wr - hi * wi, hr * wi + hi * wr], axis=0)
        query_t[:, at] = q.astype(bf16)
        query[t] = q.T.astype(bf16)
        hot_t = hot(tail_ref[pl.ds(t, 1), :], rows + hubs)
        hot_tail[:, at] = hot_t
        picked[:, at] = dot(hub_ref[...], hot_t[rows:]).astype(bf16)

    def pairs(step):
        def body(i, _):
            step(2 * i)
            step(2 * i + 1)
            return 0

        lax.fori_loop(0, tiles // 2, body, 0)

    for t in range(tiles):
        weight_of(t)
    pairs(prepare)

    def wait_rows(part):
        for o in other_groups:
            ent_copy(part, o, o).wait_recv()
        table[:, lanes_of(part)] = peers[part][partner]

    partner = match_ref[g]

    def pick(part, t):
        at = lanes_at(t)
        found = dot(table[:, lanes_of(part)], hot_tail[lanes_of(part), at])
        return (found + picked[:, at].astype(f32)).astype(bf16)

    for part in range(parts - 1):
        wait_rows(part)

        def add_part(t, part=part):
            picked[:, lanes_at(t)] = pick(part, t)

        pairs(add_part)
    wait_rows(parts - 1)

    def one_tile(t):
        at = lanes_at(t)
        tail = pick(parts - 1, t)
        scores = dot(query[t], tail)
        expo = jnp.exp(scores - jnp.max(scores, axis=1, keepdims=True))
        probs = expo * (1.0 / jnp.sum(expo, axis=1, keepdims=True))
        eye = lax.broadcasted_iota(jnp.int32, (edge, edge), 0) == lax.broadcasted_iota(
            jnp.int32, (edge, edge), 1)
        diff = jnp.where(eye, probs - 1.0, probs).astype(bf16)
        d_tail[:, at] = dot(query_t[:, at], diff).astype(bf16)
        dq = dot_last(tail, diff)
        wr, wi = halves(t)
        dr, di = dq[:half], dq[half:]
        d_head[:, at] = jnp.concatenate(
            [dr * wr + di * wi, di * wr - dr * wi], axis=0).astype(bf16)

    pairs(one_tile)

    def back_copy(part, o, slot):
        return remote(back[part].at[slot], back[part].at[slot],
                      back_send.at[part, o], back_recv.at[part, slot], (o, m))

    def send_back(part, acc):
        back[part][g] = acc.astype(bf16)
        for o in other_groups:
            back_copy(part, o, g).start()

    last = parts - 1
    acc = dot_last(d_tail[...], hot_tail[last * part_rows :, :])
    send_back(last, acc[:, :part_rows])
    for c in range(chunks):
        piece = acc[c * CHUNK_ROWS : (c + 1) * CHUNK_ROWS, part_rows:]
        if piece.shape[0] < CHUNK_ROWS:
            piece = jnp.concatenate(
                [piece, jnp.zeros((CHUNK_ROWS - piece.shape[0], hubs), f32)], axis=0)
        hub_send[c] = piece.astype(bf16)

    owner = m < chunks

    for o in other_members:
        @pl.when(o < chunks)
        def _(o=o):
            remote(hub_send.at[o], hub_in.at[m], s1.at[o], r1.at[m], (g, o)).start()

    @pl.when(owner)
    def _():
        hub_in[m] = hub_send[m]

    for part in range(last):
        send_back(part, dot_last(d_tail[...], hot_tail[lanes_of(part), :]))

    def stage_two(o, slot):
        return remote(hub_mid.at[slot], hub_mid.at[slot], s2.at[o], r2.at[slot], (o, m))

    @pl.when(owner)
    def _():
        for o in other_members:
            remote(hub_send.at[m], hub_in.at[o], s1.at[o], r1.at[o], (g, o)).wait_recv()
        total = hub_in[0].astype(f32)
        for i in range(1, members):
            total = total + hub_in[i].astype(f32)
        hub_mid[g] = total
        for o in other_groups:
            stage_two(o, g).start()

    head_sum[...] = dot_last(d_head[...], hot_head[...])

    def stage_three(o, slot):
        return remote(hub_out.at[slot], hub_out.at[slot], s3.at[o], r3.at[slot], (g, o))

    @pl.when(owner)
    def _():
        for o in other_groups:
            stage_two(o, o).wait_recv()
        total = hub_mid[0]
        for i in range(1, groups):
            total = total + hub_mid[i]
        hub_out[m] = (hub_pad[m] - learn_rate * total).astype(bf16)
        for o in other_members:
            stage_three(o, m).start()

    source = jnp.int32(0)
    for i in range(1, groups):
        source = jnp.where(match_ref[i] == g, i, source)
    for part in [last, *range(last)]:
        for o in other_groups:
            back_copy(part, o, o).wait_recv()
        at = lanes_of(part)
        grads = head_sum[:, at] + back[part][source].astype(f32)
        new_ent_ref[:, at] = (ent_ref[:, at].astype(f32) - learn_rate * grads).astype(bf16)

    for o in other_members:
        @pl.when(o < chunks)
        def _(o=o):
            stage_three(o, o).wait_recv()
    new_hub_ref[...] = hub_out[...].reshape(chunks * CHUNK_ROWS, hubs)[:width]

    for part in range(parts):
        for o in other_groups:
            ent_copy(part, o, g).wait_send()
            back_copy(part, o, g).wait_send()
    for o in other_members:
        @pl.when(o < chunks)
        def _(o=o):
            remote(hub_send.at[o], hub_in.at[m], s1.at[o], r1.at[m], (g, o)).wait_send()

    @pl.when(owner)
    def _():
        for o in other_groups:
            stage_two(o, g).wait_send()
        for o in other_members:
            stage_three(o, m).wait_send()


def shards(groups, members, entities, hub_rows, relations, matching, head_index, tail_index, tile_rel, tile_count):
    rows, width = entities.shape
    hubs = hub_rows.shape[0]
    tiles, edge = head_index.shape
    edges = tiles * edge
    chunks = -(-width // CHUNK_ROWS)
    blocks = -(-relations.shape[0] // LANES)
    parts = 2
    smem = pl.BlockSpec(memory_space=pltpu.SMEM)
    vmem = pl.BlockSpec(memory_space=pltpu.VMEM)
    dma = pltpu.SemaphoreType.DMA
    new_ent, new_hub = pl.pallas_call(
        functools.partial(kernel, groups, members),
        out_shape=(
            jax.ShapeDtypeStruct((width, rows), bf16),
            jax.ShapeDtypeStruct((width, hubs), bf16),
        ),
        in_specs=[smem, smem, smem, vmem, vmem, vmem, vmem, pl.BlockSpec(memory_space=pl.ANY)],
        out_specs=(vmem, vmem),
        scratch_shapes=[
            pltpu.VMEM((width, relations.shape[0]), f32),
            pltpu.VMEM((blocks, width, LANES), f32),
            pltpu.VMEM((groups, width, rows // parts), bf16),
            pltpu.VMEM((groups, width, rows // parts), bf16),
            pltpu.VMEM((width, rows), bf16),
            pltpu.VMEM((tiles, width, LANES), f32),
            pltpu.VMEM((rows, edges), bf16),
            pltpu.VMEM((rows + hubs, edges), bf16),
            pltpu.VMEM((width, edges), bf16),
            pltpu.VMEM((width, edges), bf16),
            pltpu.VMEM((tiles, edge, width), bf16),
            pltpu.VMEM((width, edges), bf16),
            pltpu.VMEM((width, edges), bf16),
            pltpu.VMEM((groups, width, rows // parts), bf16),
            pltpu.VMEM((groups, width, rows // parts), bf16),
            pltpu.VMEM((width, rows), f32),
            pltpu.VMEM((chunks, CHUNK_ROWS, hubs), f32),
            pltpu.VMEM((chunks, CHUNK_ROWS, hubs), bf16),
            pltpu.VMEM((members, CHUNK_ROWS, hubs), bf16),
            pltpu.VMEM((groups, CHUNK_ROWS, hubs), f32),
            pltpu.VMEM((chunks, CHUNK_ROWS, hubs), bf16),
            dma,
            dma((parts, groups)),
            dma((parts, groups)),
            dma((parts, groups)),
            dma((parts, groups)),
            dma((members,)),
            dma((members,)),
            dma((groups,)),
            dma((groups,)),
            dma((members,)),
            dma((members,)),
        ],
        compiler_params=pltpu.CompilerParams(
            collective_id=0, has_side_effects=True, vmem_limit_bytes=58 * 1024 * 1024
        ),
        cost_estimate=pl.CostEstimate(
            flops=4 * edges * width * (2 * rows + hubs + edge),
            bytes_accessed=relations.size * 4,
            transcendentals=edges * edge),
    )(tile_count, tile_rel, matching, entities.T, hub_rows.T, head_index, tail_index, relations.T)
    return new_ent.T, new_hub.T


def solution(mesh):
    placed = (
        P(("group", "member"), None),
        P(),
        P(),
        P(),
        P(("group", "member"), None),
        P(("group", "member"), None),
        P(("group", "member")),
        P("group", "member"),
    )
    return jax.shard_map(
        functools.partial(shards, mesh.shape["group"], mesh.shape["member"]),
        mesh=mesh,
        in_specs=placed,
        out_specs=(P(("group", "member"), None), P()),
        check_vma=False,
    )
```

time: 65.8 us -> 53.6 us (0.81)
  local copies, waits for them, and re-layouts: 12.5 us -> 3.32 us
  Pallas kernels: 51.6 us -> 48.7 us
    unnamed x3 -> x2, local copies, waits for them, and re-layouts: 8.91 us -> 3.32 us
    pallas_call x2 -> x0, local copies, waits for them, and re-layouts: 3.63 us -> none  [shards(): pl.pallas_call(functools.partial(kernel, groups, members), out_shape=(jax...]
    pallas_call x1, Pallas kernels: 51.6 us -> 48.7 us  [shards(): pl.pallas_call(functools.partial(kernel, groups, members), out_shape=(jax...]
where the time goes in v2:
time: 53.6 us; the launch traced here: 53.3 us
  Pallas kernels  48.7 us (91%)
  local copies, waits for them, and re-layouts  3.32 us (6%)
  between operations  1.29 us (2%)
    pallas_call x1, Pallas kernels, shards(): pl.pallas_call(functools.partial(kernel, groups, members), out_shape=(jax...  48.7 us
    unnamed x2, local copies, waits for them, and re-layouts  3.32 us

profile of v2, /device:TPU:0, one launch (start us, length us, event | category | flops | bytes accessed | tf_op | source)
XLA Modules:
  0.0 53.3 jit_solution(3184588094037031376)
XLA Ops:
  1.3 48.7 %shard_map.95 = (bf16[400,512]{1,0:T(8,128)(2,1)}, bf16[400,128]{1,0:T(8,128)(2,1)}) custom-call(s32[1,1]{1,0:T(1,128)S(6)} %copy.12.count_ref, s32[16]{0:T(128)} %rel_ref.1, s32[2]{0:T(128)} %match_ref.1, bf16[400,512]{1,0:T(8,128)(2,1)} %bitcast.8, bf16[400,128]{1,0:T(8,128)(2,1)} %bitcast.9, s32[16,256]{1,0:T(8,128)} %head_ref.1, s32[16,256]{1,0:T(8,128)} %tail_ref.1, ...), custom_call_target="tpu_custom_call" | custom-call | flops 9227468800 | bytes 3379200 | tf_op jit(solution)/shard_map/pallas_call | solution.py:289
  50.0 1.8 %copy.13 = bf16[512,400]{0,1:T(8,128)(2,1)} copy(bf16[512,400]{0,1:T(8,128)(2,1)} %bitcast.5) | data formatting | bytes 819200
  51.8 1.5 %copy.14 = bf16[128,400]{0,1:T(8,128)(2,1)} copy(bf16[128,400]{0,1:T(8,128)(2,1)} %bitcast.6) | data formatting | bytes 204800

commit v3 on v2

--- a/solution.py
+++ b/solution.py
@@ -11,6 +11,7 @@
 MESH = pl.DeviceIdType.MESH
 LANES = 128
 CHUNK_ROWS = 32
+UNROLL = 4
 contract_last = (((1,), (1,)), ((), ()))
 f32 = jnp.float32
 bf16 = jnp.bfloat16
@@ -128,17 +129,17 @@
         hot_tail[:, at] = hot_t
         picked[:, at] = dot(hub_ref[...], hot_t[rows:]).astype(bf16)
 
-    def pairs(step):
+    def quads(step):
         def body(i, _):
-            step(2 * i)
-            step(2 * i + 1)
+            for k in range(UNROLL):
+                step(UNROLL * i + k)
             return 0
 
-        lax.fori_loop(0, tiles // 2, body, 0)
+        lax.fori_loop(0, tiles // UNROLL, body, 0)
 
     for t in range(tiles):
         weight_of(t)
-    pairs(prepare)
+    quads(prepare)
 
     def wait_rows(part):
         for o in other_groups:
@@ -158,7 +159,7 @@
         def add_part(t, part=part):
             picked[:, lanes_at(t)] = pick(part, t)
 
-        pairs(add_part)
+        quads(add_part)
     wait_rows(parts - 1)
 
     def one_tile(t):
@@ -177,7 +178,7 @@
         d_head[:, at] = jnp.concatenate(
             [dr * wr + di * wi, di * wr - dr * wi], axis=0).astype(bf16)
 
-    pairs(one_tile)
+    quads(one_tile)
 
     def back_copy(part, o, slot):
         return remote(back[part].at[slot], back[part].at[slot],
@@ -273,6 +274,11 @@
             stage_two(o, g).wait_send()
         for o in other_members:
             stage_three(o, m).wait_send()
+
+
+def hand_over(ent_ref, hub_ref, new_ent_ref, new_hub_ref):
+    new_ent_ref[...] = ent_ref[...]
+    new_hub_ref[...] = hub_ref[...]
 
 
 def shards(groups, members, entities, hub_rows, relations, matching, head_index, tail_index, tile_rel, tile_count):
@@ -336,6 +342,15 @@
             bytes_accessed=relations.size * 4,
             transcendentals=edges * edge),
     )(tile_count, tile_rel, matching, entities.T, hub_rows.T, head_index, tail_index, relations.T)
+    new_ent, new_hub = pl.pallas_call(
+        hand_over,
+        out_shape=(
+            jax.ShapeDtypeStruct(new_ent.shape, bf16),
+            jax.ShapeDtypeStruct(new_hub.shape, bf16),
+        ),
+        in_specs=[vmem, vmem],
+        out_specs=(vmem, vmem),
+    )(new_ent, new_hub)
     return new_ent.T, new_hub.T
 
 

time: 53.6 us -> 51.3 us (0.957)
  local copies, waits for them, and re-layouts: 3.32 us -> 0 us
  Pallas kernels: 48.7 us -> 49.9 us
    unnamed x2 -> x0, local copies, waits for them, and re-layouts: 3.32 us -> none
    pallas_call x0 -> x1, Pallas kernels: none -> 1.82 us  [shards(): pl.pallas_call(hand_over, out_shape=(jax.ShapeDtypeStruct(new_ent.shape,...]
    pallas_call x1, Pallas kernels: 48.7 us -> 48.1 us  [shards(): pl.pallas_call(functools.partial(kernel, groups, members), out_shape=(jax...]
where the time goes in v3:
time: 51.3 us; the launch traced here: 51.2 us
  Pallas kernels  49.9 us (97%)
  between operations  1.29 us (3%)
    pallas_call x1, Pallas kernels, shards(): pl.pallas_call(functools.partial(kernel, groups, members), out_shape=(jax...  48.1 us
    pallas_call x1, Pallas kernels, shards(): pl.pallas_call(hand_over, out_shape=(jax.ShapeDtypeStruct(new_ent.shape,...  1.82 us

profile of v3, /device:TPU:0, one launch (start us, length us, event | category | flops | bytes accessed | tf_op | source)
XLA Modules:
  0.0 51.2 jit_solution(5388054396066035487)
XLA Ops:
  1.3 48.1 %shard_map.95 = (bf16[400,512]{1,0:T(8,128)(2,1)}, bf16[400,128]{1,0:T(8,128)(2,1)}) custom-call(s32[1,1]{1,0:T(1,128)S(6)} %copy.10.count_ref, s32[16]{0:T(128)} %rel_ref.1, s32[2]{0:T(128)} %match_ref.1, bf16[400,512]{1,0:T(8,128)(2,1)} %bitcast.6, bf16[400,128]{1,0:T(8,128)(2,1)} %bitcast.8, s32[16,256]{1,0:T(8,128)} %head_ref.1, s32[16,256]{1,0:T(8,128)} %tail_ref.1, ...), custom_call_target="tpu_custom_call" | custom-call | flops 9227468800 | bytes 3379200 | tf_op jit(solution)/shard_map/pallas_call | solution.py:295
  49.3 1.8 %shard_map.96 = (bf16[400,512]{1,0:T(8,128)(2,1)}, bf16[400,128]{1,0:T(8,128)(2,1)}) custom-call(bf16[400,512]{1,0:T(8,128)(2,1)} %get-tuple-element.6.ent_ref, bf16[400,128]{1,0:T(8,128)(2,1)} %get-tuple-element.7.hub_ref), custom_call_target="tpu_custom_call" | custom-call | tf_op jit(solution)/shard_map/pallas_call | solution.py:345

commit v4 on v3

--- a/solution.py
+++ b/solution.py
@@ -31,6 +31,7 @@
     new_ent_ref, new_hub_ref,
     landed, relations, peers_0, peers_1, table, weights, hot_head, hot_tail, picked,
     query_t, query, d_head, d_tail, back_0, back_1, head_sum,
+    scores_0, scores_1, diff_0, diff_1,
     hub_pad, hub_send, hub_in, hub_mid, hub_out,
     rel_sem, ent_send, ent_recv, back_send, back_recv,
     s1, r1, s2, r2, s3, r3,
@@ -43,6 +44,7 @@
     tiles, edge = head_ref.shape
     rels = table_ref.shape[1]
     peers, back = (peers_0, peers_1), (back_0, back_1)
+    scores_of, diff_of = (scores_0, scores_1), (diff_0, diff_1)
     parts = len(back)
     part_rows = rows // parts
     chunks = hub_send.shape[0]
@@ -98,6 +100,9 @@
     def lanes_at(t):
         return pl.ds(pl.multiple_of(t * edge, edge), edge)
 
+    def wide_at(t):
+        return pl.ds(pl.multiple_of(t * edge, UNROLL * edge), UNROLL * edge)
+
     def hot(ids, n):
         return (lax.broadcasted_iota(jnp.int32, (n, edge), 0) == ids).astype(f32).astype(bf16)
 
@@ -115,24 +120,28 @@
         w = jnp.concatenate([weights[t]] * (edge // LANES), axis=1)
         return w[:half], w[half:]
 
-    def prepare(t):
-        at = lanes_at(t)
-        hot_h = hot(head_ref[pl.ds(t, 1), :], rows)
-        hot_head[:, at] = hot_h
-        head = dot(ent_ref[...], hot_h)
-        wr, wi = halves(t)
-        hr, hi = head[:half], head[half:]
-        q = jnp.concatenate([hr * wr - hi * wi, hr * wi + hi * wr], axis=0)
-        query_t[:, at] = q.astype(bf16)
-        query[t] = q.T.astype(bf16)
-        hot_t = hot(tail_ref[pl.ds(t, 1), :], rows + hubs)
-        hot_tail[:, at] = hot_t
-        picked[:, at] = dot(hub_ref[...], hot_t[rows:]).astype(bf16)
+    def prepare(first):
+        group = [first + k for k in range(UNROLL)]
+        for t in group:
+            hot_head[:, lanes_at(t)] = hot(head_ref[pl.ds(t, 1), :], rows)
+        found = [dot(ent_ref[...], hot_head[:, lanes_at(t)]) for t in group]
+        for t in group:
+            hot_tail[:, lanes_at(t)] = hot(tail_ref[pl.ds(t, 1), :], rows + hubs)
+        queries = []
+        for t, head in zip(group, found):
+            wr, wi = halves(t)
+            hr, hi = head[:half], head[half:]
+            q = jnp.concatenate([hr * wr - hi * wi, hr * wi + hi * wr], axis=0)
+            query_t[:, lanes_at(t)] = q.astype(bf16)
+            queries.append(q)
+        for t, q in zip(group, queries):
+            query[t] = q.T.astype(bf16)
+        at = wide_at(first)
+        picked[:, at] = dot(hub_ref[...], hot_tail[rows:, at]).astype(bf16)
 
     def quads(step):
         def body(i, _):
-            for k in range(UNROLL):
-                step(UNROLL * i + k)
+            step(UNROLL * i)
             return 0
 
         lax.fori_loop(0, tiles // UNROLL, body, 0)
@@ -148,37 +157,52 @@
 
     partner = match_ref[g]
 
-    def pick(part, t):
-        at = lanes_at(t)
-        found = dot(table[:, lanes_of(part)], hot_tail[lanes_of(part), at])
-        return (found + picked[:, at].astype(f32)).astype(bf16)
-
-    for part in range(parts - 1):
+    for part in range(parts):
         wait_rows(part)
 
-        def add_part(t, part=part):
-            picked[:, lanes_at(t)] = pick(part, t)
+        def add_part(first, part=part):
+            at = wide_at(first)
+            found = dot(table[:, lanes_of(part)], hot_tail[lanes_of(part), at])
+            picked[:, at] = (found + picked[:, at].astype(f32)).astype(bf16)
 
         quads(add_part)
-    wait_rows(parts - 1)
-
-    def one_tile(t):
-        at = lanes_at(t)
-        tail = pick(parts - 1, t)
-        scores = dot(query[t], tail)
+
+    def make_scores(t, par):
+        scores_of[par][...] = dot(query[t], picked[:, lanes_at(t)])
+
+    def make_diff(par):
+        scores = scores_of[par][...]
         expo = jnp.exp(scores - jnp.max(scores, axis=1, keepdims=True))
         probs = expo * (1.0 / jnp.sum(expo, axis=1, keepdims=True))
         eye = lax.broadcasted_iota(jnp.int32, (edge, edge), 0) == lax.broadcasted_iota(
             jnp.int32, (edge, edge), 1)
-        diff = jnp.where(eye, probs - 1.0, probs).astype(bf16)
+        diff_of[par][...] = jnp.where(eye, probs - 1.0, probs).astype(bf16)
+
+    def make_grads(t, par):
+        at = lanes_at(t)
+        diff = diff_of[par][...]
         d_tail[:, at] = dot(query_t[:, at], diff).astype(bf16)
-        dq = dot_last(tail, diff)
+        dq = dot_last(picked[:, at], diff)
         wr, wi = halves(t)
         dr, di = dq[:half], dq[half:]
         d_head[:, at] = jnp.concatenate(
             [dr * wr + di * wi, di * wr - dr * wi], axis=0).astype(bf16)
 
-    quads(one_tile)
+    def two_steps(i, _):
+        for par in range(2):
+            t = 2 * i + par
+            make_scores(t, par)
+            make_diff(1 - par)
+            make_grads(t - 2, par)
+        return 0
+
+    make_scores(0, 0)
+    make_scores(1, 1)
+    make_diff(0)
+    lax.fori_loop(1, tiles // 2, two_steps, 0)
+    make_diff(1)
+    make_grads(tiles - 2, 0)
+    make_grads(tiles - 1, 1)
 
     def back_copy(part, o, slot):
         return remote(back[part].at[slot], back[part].at[slot],
@@ -317,6 +341,10 @@
             pltpu.VMEM((groups, width, rows // parts), bf16),
             pltpu.VMEM((groups, width, rows // parts), bf16),
             pltpu.VMEM((width, rows), f32),
+            pltpu.VMEM((edge, edge), f32),
+            pltpu.VMEM((edge, edge), f32),
+            pltpu.VMEM((edge, edge), bf16),
+            pltpu.VMEM((edge, edge), bf16),
             pltpu.VMEM((chunks, CHUNK_ROWS, hubs), f32),
             pltpu.VMEM((chunks, CHUNK_ROWS, hubs), bf16),
             pltpu.VMEM((members, CHUNK_ROWS, hubs), bf16),

time: 51.3 us -> 45.9 us (0.89)
  Pallas kernels: 49.9 us -> 44.5 us
    pallas_call x1, Pallas kernels: 48.1 us -> 42.6 us  [shards(): pl.pallas_call(functools.partial(kernel, groups, members), out_shape=(jax...]
where the time goes in v4:
time: 45.9 us; the launch traced here: 45.7 us
  Pallas kernels  44.5 us (97%)
  between operations  1.29 us (3%)
    pallas_call x1, Pallas kernels, shards(): pl.pallas_call(functools.partial(kernel, groups, members), out_shape=(jax...  42.6 us
    pallas_call x1, Pallas kernels, shards(): pl.pallas_call(hand_over, out_shape=(jax.ShapeDtypeStruct(new_ent.shape,...  1.82 us

profile of v4, /device:TPU:0, one launch (start us, length us, event | category | flops | bytes accessed | tf_op | source)
XLA Modules:
  0.0 45.7 jit_solution(15834499236225251630)
XLA Ops:
  1.3 42.6 %shard_map.95 = (bf16[400,512]{1,0:T(8,128)(2,1)}, bf16[400,128]{1,0:T(8,128)(2,1)}) custom-call(s32[1,1]{1,0:T(1,128)S(6)} %copy.10.count_ref, s32[16]{0:T(128)} %rel_ref.1, s32[2]{0:T(128)} %match_ref.1, bf16[400,512]{1,0:T(8,128)(2,1)} %bitcast.6, bf16[400,128]{1,0:T(8,128)(2,1)} %bitcast.8, s32[16,256]{1,0:T(8,128)} %head_ref.1, s32[16,256]{1,0:T(8,128)} %tail_ref.1, ...), custom_call_target="tpu_custom_call" | custom-call | flops 9227468800 | bytes 3379200 | tf_op jit(solution)/shard_map/pallas_call | solution.py:319
  43.9 1.8 %shard_map.96 = (bf16[400,512]{1,0:T(8,128)(2,1)}, bf16[400,128]{1,0:T(8,128)(2,1)}) custom-call(bf16[400,512]{1,0:T(8,128)(2,1)} %get-tuple-element.6.ent_ref, bf16[400,128]{1,0:T(8,128)(2,1)} %get-tuple-element.7.hub_ref), custom_call_target="tpu_custom_call" | custom-call | tf_op jit(solution)/shard_map/pallas_call | solution.py:373
